TPU v7x, 128 devices: a whole 4x4x4 slice. The times are simulated.
128 devices in a mesh: expert: 64 (over z, y, x), node: 2 (over core).
Axes of the slice: x: 4, y: 4, z: 4, core: 2. Of those that a mesh axis runs over, the one named last changes fastest.
Arguments:
- samples: bfloat16 [98304, 512], P(('expert', 'node')), may hold values from -6 to 6
- cotangent: bfloat16 [98304, 512], P(('expert', 'node')), may hold values from -6 to 6
- weights: bfloat16 [256, 2, 512, 512], P('expert', None, 'node'), may hold values from -0.25 to 0.25
- expert_ids: int32 [98304, 1], P(('expert', 'node')), may hold values from 0 to 255; in each aligned block of 768 rows (0 to 767, 768 to 1535, ...) at most 6 rows name the same one
Outputs:
- sample_grads: bfloat16 [98304, 512], P(('expert', 'node'))
- weight_grads: bfloat16 [256, 2, 512, 512], P('expert', None, 'node')
Inputs may be any that keep to these rules, and one draw needn't show every extreme that they name: `expert_ids`: among the samples of one device no expert is named more than 6 times, and in some device's samples one expert is named exactly 6 times.
All inputs are finite; a program needn't handle non-finite values.
Results may differ from a plain program's by a relative error of at most 0.015.
Values may be sent and summed in bfloat16 or wider, within the bound.
A program may use at most 64 MiB of HBM per device.

v0:
```python
import math

import jax
import jax.numpy as jnp
from jax import lax
from jax.sharding import PartitionSpec as P


def silu_slope(preact):
    sigmoid_val = jax.nn.sigmoid(preact)
    return sigmoid_val * (1.0 + preact * (1.0 - sigmoid_val))


def on_device(samples, cotangent, weights, expert_ids):
    row_count, feat_count = samples.shape
    local_count = weights.shape[0]
    layer_count = weights.shape[1]
    owner_count = lax.axis_size("expert")
    node_count = lax.axis_size("node")
    expert_count = local_count * owner_count
    capacity = 2 * row_count // expert_count
    buffer_rows = expert_count * capacity
    full_weights = lax.all_gather(weights, "node", axis=2, tiled=True)
    expert_of = expert_ids[:, 0]
    columns = lax.broadcasted_iota(jnp.int32, (row_count, expert_count), 1)
    onehot = (expert_of[:, None] == columns).astype(jnp.bfloat16)
    row_pos = lax.broadcasted_iota(jnp.int32, (row_count, row_count), 0)
    col_pos = lax.broadcasted_iota(jnp.int32, (row_count, row_count), 1)
    strictly_lower = (col_pos < row_pos).astype(jnp.bfloat16)
    earlier = jnp.dot(strictly_lower, onehot, preferred_element_type=jnp.float32)
    slot_of = jnp.sum(earlier * onehot.astype(jnp.float32), axis=1).astype(jnp.int32)
    owner_of = expert_of // local_count
    local_of = expert_of % local_count
    target = (local_of * owner_count + owner_of) * capacity + slot_of
    source = (
        jnp.full((buffer_rows,), row_count, jnp.int32)
        .at[target]
        .set(jnp.arange(row_count, dtype=jnp.int32))
    )
    zero_row = jnp.zeros((1, feat_count), samples.dtype)
    feats_buf = jnp.concatenate([samples, zero_row], 0)[source].reshape(
        local_count, owner_count, capacity, feat_count
    )
    cots_buf = jnp.concatenate([cotangent, zero_row], 0)[source].reshape(
        local_count, owner_count, capacity, feat_count
    )
    feats_in, cots_in = (
        lax.all_to_all(feats_buf, "expert", split_axis=1, concat_axis=1, tiled=True),
        lax.all_to_all(cots_buf, "expert", split_axis=1, concat_axis=1, tiled=True),
    )
    feats_in = feats_in.reshape(local_count, owner_count * capacity, feat_count)
    cots_in = cots_in.reshape(local_count, owner_count * capacity, feat_count)
    acts = [feats_in]
    preacts = []
    for layer in range(layer_count):
        preact = jnp.einsum(
            "lrd,ldk->lrk", acts[-1], full_weights[:, layer], preferred_element_type=jnp.float32
        )
        preacts.append(preact)
        if layer < layer_count - 1:
            acts.append(jax.nn.silu(preact).astype(jnp.bfloat16))
    norm_scale = 1.0 / math.sqrt(row_count * node_count / local_count)
    grad = cots_in
    partials = [None] * layer_count
    for layer in reversed(range(layer_count)):
        pre_grad = (grad.astype(jnp.float32) * silu_slope(preacts[layer])).astype(jnp.bfloat16)
        partials[layer] = (
            jnp.einsum("lrd,lrk->ldk", acts[layer], pre_grad, preferred_element_type=jnp.float32)
            * norm_scale
        )
        grad = jnp.einsum(
            "lrk,ldk->lrd", pre_grad, full_weights[:, layer], preferred_element_type=jnp.float32
        ).astype(jnp.bfloat16)
    returned = lax.all_to_all(
        grad.reshape(local_count, owner_count, capacity, feat_count),
        "expert",
        split_axis=1,
        concat_axis=1,
        tiled=True,
    )
    sample_grads = returned.reshape(buffer_rows, feat_count)[target]
    partial_value = jnp.stack(partials, 1)
    share_rows = feat_count // node_count
    summed = lax.psum(partial_value.astype(jnp.bfloat16), "node").astype(jnp.float32)
    summed = lax.dynamic_slice_in_dim(summed, lax.axis_index("node") * share_rows, share_rows, 2)
    return (sample_grads, summed.astype(jnp.bfloat16))


def solution(mesh):
    return jax.shard_map(
        on_device,
        mesh=mesh,
        in_specs=(
            P(("expert", "node"), None),
            P(("expert", "node"), None),
            P("expert", None, "node", None),
            P(("expert", "node"), None),
        ),
        out_specs=(P(("expert", "node"), None), P("expert", None, "node", None)),
        check_vma=False,
    )
```

profile of v0, /device:TPU:0, one launch (start us, length us, event | category | flops | bytes accessed | tf_op | source)
XLA Modules:
  0.0 157.2 jit_solution(13782548362484772422)
XLA Ops:
  7.2 3.0 %copy.22 = bf16[4,2,256,512]{3,2,0,1:T(8,128)(2,1)} copy(bf16[4,2,256,512]{3,2,1,0:T(8,128)(2,1)} %param.6) | data formatting | bytes 4194304 | tf_op args[2]
  11.5 3.4 %scatter_custom_fusion = s32[1536]{0:T(1024)S(1)} fusion(s32[768]{0:T(1024)S(1)} %fusion.16, s32[768]{0:T(1024)S(1)} %iota.21, s32[]{:T(128)} %constant.21.clone.1), kind=kCustom, calls=%fused_computation.40 | custom fusion | bytes 6148 | tf_op jit(solution)/shard_map/scatter | solution.py:38
  14.9 5.4 %gather_fusion.1 = bf16[1536,512]{1,0:T(8,128)(2,1)} fusion(bf16[769,512]{1,0:T(8,128)(2,1)S(1)} %concatenate.7, s32[2048]{0:T(1024)S(1)} %pad_clamp_fusion), kind=kCustom, calls=%fused_computation.1 | custom fusion | bytes 3151872 | tf_op jit(solution)/shard_map/gather | solution.py:41
  20.4 2.5 %reshape.31 = bf16[4,64,6,512]{3,2,1,0:T(8,128)(2,1)S(1)} reshape(bf16[1536,512]{1,0:T(8,128)(2,1)} %gather_fusion.1) | data formatting | bytes 3145728 | tf_op jit(solution)/shard_map/reshape | solution.py:41
  22.9 3.2 %copy.21 = bf16[4,64,6,512]{3,0,2,1:T(4,128)(2,1)} copy(bf16[4,64,6,512]{3,2,1,0:T(8,128)(2,1)S(1)} %reshape.31) | data formatting | bytes 3145728 | tf_op jit(solution)/shard_map/reshape | solution.py:41
  26.1 11.9 %all-to-all-start.1 = ((bf16[4,64,6,512]{3,0,2,1:T(4,128)(2,1)}), bf16[4,64,6,512]{3,0,2,1:T(4,128)(2,1)}, u32[]{:S(2)}, u32[]{:S(2)}) async-start(bf16[4,64,6,512]{3,0,2,1:T(4,128)(2,1)} %copy.21), calls=%async_computation.1 | async-start | bytes 3145728 | tf_op jit(solution)/shard_map/all_to_all | solution.py:48
  38.1 5.5 %gather_fusion = bf16[1536,512]{1,0:T(8,128)(2,1)} fusion(bf16[769,512]{1,0:T(8,128)(2,1)S(1)} %concatenate.6, s32[2048]{0:T(1024)S(1)} %pad_clamp_fusion), kind=kCustom, calls=%fused_computation | custom fusion | bytes 3151872 | tf_op jit(solution)/shard_map/gather | solution.py:44
  43.6 2.5 %reshape.30 = bf16[4,64,6,512]{3,2,1,0:T(8,128)(2,1)S(1)} reshape(bf16[1536,512]{1,0:T(8,128)(2,1)} %gather_fusion) | data formatting | bytes 3145728 | tf_op jit(solution)/shard_map/reshape | solution.py:44
  46.1 3.3 %copy.20 = bf16[4,64,6,512]{3,0,2,1:T(4,128)(2,1)} copy(bf16[4,64,6,512]{3,2,1,0:T(8,128)(2,1)S(1)} %reshape.30) | data formatting | bytes 3145728 | tf_op jit(solution)/shard_map/reshape | solution.py:44
  49.3 13.0 %all-to-all-done.1 = bf16[4,64,6,512]{3,0,2,1:T(4,128)(2,1)} async-done(((bf16[4,64,6,512]{3,0,2,1:T(4,128)(2,1)}), bf16[4,64,6,512]{3,0,2,1:T(4,128)(2,1)}, u32[]{:S(2)}, u32[]{:S(2)}) %all-to-all-start.1) | async-done | bytes 1572896 | tf_op jit(solution)/shard_map/all_to_all | solution.py:48
  62.4 5.1 %all-to-all-start = ((bf16[4,64,6,512]{3,0,2,1:T(4,128)(2,1)}), bf16[4,64,6,512]{3,0,2,1:T(4,128)(2,1)S(1)}, u32[]{:S(2)}, u32[]{:S(2)}) async-start(bf16[4,64,6,512]{3,0,2,1:T(4,128)(2,1)} %copy.20), calls=%async_computation | async-start | bytes 3145728 | tf_op jit(solution)/shard_map/all_to_all | solution.py:49
  67.7 3.0 %copy.27 = bf16[4,384,512]{1,2,0:T(8,128)(2,1)S(1)} copy(bf16[4,384,512]{2,0,1:T(4,128)(2,1)} %bitcast.1) | data formatting | bytes 3145728 | tf_op jit(solution)/shard_map/reshape | solution.py:51
  70.8 19.8 %all-to-all-done = bf16[4,64,6,512]{3,0,2,1:T(4,128)(2,1)S(1)} async-done(((bf16[4,64,6,512]{3,0,2,1:T(4,128)(2,1)}), bf16[4,64,6,512]{3,0,2,1:T(4,128)(2,1)S(1)}, u32[]{:S(2)}, u32[]{:S(2)}) %all-to-all-start) | async-done | bytes 1572896 | tf_op jit(solution)/shard_map/all_to_all | solution.py:49
  90.6 2.3 %bitcast_convert_fusion = f32[4,384,512]{2,0,1:T(4,128)} fusion(bf16[4,64,6,512]{3,0,2,1:T(4,128)(2,1)S(1)} %all-to-all-done), kind=kLoop, calls=%fused_computation.25 | loop fusion | flops 786432 | bytes 4718592 | tf_op jit(solution)/shard_map/convert_element_type | solution.py:66
  92.9 2.8 %fusion.3 = f32[4,384,512]{2,1,0:T(8,128)S(1)} fusion(bf16[4,384,512]{1,2,0:T(8,128)(2,1)S(1)} %copy.27, bf16[4,2,512,512]{3,2,0,1:T(8,128)(2,1)} %all-gather.2.cloned.1.call-done), kind=kOutput, calls=%fused_computation.18 | convolution fusion | flops 805306368 | bytes 6815744 | tf_op jit(solution)/shard_map/lrd,ldk->lrk/dot_general | solution.py:56
  95.6 4.2 %fusion = bf16[4,384,512]{2,1,0:T(8,128)(2,1)S(1)} fusion(f32[4,384,512]{2,0,1:T(4,128)S(1)} %copy-done, bf16[4,2,512,512]{3,2,0,1:T(8,128)(2,1)} %all-gather.2.cloned.1.call-done, f32[4,384,512]{2,1,0:T(8,128)S(1)} %fusion.3), kind=kOutput, calls=%fused_computation.9 | convolution fusion | flops 816316416 | bytes 9961472 | tf_op jit(solution)/shard_map/lrd,ldk->lrk/dot_general | solution.py:56
  104.8 2.3 %pad_maximum_fusion = bf16[4,2,512,512]{3,2,0,1:T(8,128)(2,1)} fusion(bf16[4,1,512,512]{3,2,0,1:T(8,128)(2,1)S(1)} %fusion.9, bf16[4,1,512,512]{3,2,0,1:T(8,128)(2,1)S(1)} %fusion.8), kind=kLoop, calls=%fused_computation.4 | loop fusion | flops 2097152 | bytes 8388608 | tf_op jit(solution)/shard_map/stack | solution.py:82
  107.1 2.6 %fusion.7 = bf16[4,384,512]{2,1,0:T(8,128)(2,1)S(1)} fusion(bf16[4,384,512]{2,1,0:T(8,128)(2,1)S(1)} %multiply_convert_fusion.2, bf16[4,2,512,512]{3,2,0,1:T(8,128)(2,1)} %all-gather.2.cloned.1.call-done), kind=kOutput, calls=%fused_computation.22 | convolution fusion | flops 806092800 | bytes 5242880 | tf_op jit(solution)/shard_map/lrk,ldk->lrd/dot_general | solution.py:71
  109.7 2.4 %copy.25 = bf16[4,384,512]{2,0,1:T(4,128)(2,1)} copy(bf16[4,384,512]{2,1,0:T(8,128)(2,1)S(1)} %fusion.7) | data formatting | bytes 3145728 | tf_op jit(solution)/shard_map/convert_element_type | solution.py:73
  112.1 4.9 %all-to-all-start.2 = ((bf16[4,64,6,512]{3,0,2,1:T(4,128)(2,1)}), bf16[4,64,6,512]{3,0,2,1:T(4,128)(2,1)S(1)}, u32[]{:S(2)}, u32[]{:S(2)}) async-start(bf16[4,64,6,512]{3,0,2,1:T(4,128)(2,1)} %bitcast.4), calls=%async_computation.2 | async-start | bytes 3145728 | tf_op jit(solution)/shard_map/all_to_all | solution.py:74
  117.0 22.4 %all-to-all-done.2 = bf16[4,64,6,512]{3,0,2,1:T(4,128)(2,1)S(1)} async-done(((bf16[4,64,6,512]{3,0,2,1:T(4,128)(2,1)}), bf16[4,64,6,512]{3,0,2,1:T(4,128)(2,1)S(1)}, u32[]{:S(2)}, u32[]{:S(2)}) %all-to-all-start.2) | async-done | bytes 1572896 | tf_op jit(solution)/shard_map/all_to_all | solution.py:74
  141.1 2.6 %reshape.34 = bf16[1536,512]{1,0:T(8,128)(2,1)S(1)} reshape(bf16[4,64,6,512]{3,2,1,0:T(8,128)(2,1)} %copy.26) | data formatting | bytes 3145728 | tf_op jit(solution)/shard_map/reshape | solution.py:81
  143.7 3.3 %gather_fusion.2 = bf16[768,512]{1,0:T(8,128)(2,1)} fusion(bf16[1536,512]{1,0:T(8,128)(2,1)S(1)} %reshape.34, s32[1024]{0:T(1024)S(1)} %pad_clamp_fusion.1), kind=kCustom, calls=%fused_computation.2 | custom fusion | bytes 1575936 | tf_op jit(solution)/shard_map/gather | solution.py:81
  147.0 1.8 %convert_convert_fusion = bf16[4,2,256,512]{3,2,0,1:T(8,128)(2,1)S(1)} fusion(bf16[4,2,512,512]{3,2,0,1:T(8,128)(2,1)} %all-reduce.4.cloned.1.call-done, s32[]{:T(128)S(6)} %select_n.30), kind=kLoop, calls=%fused_computation.5 | loop fusion | flops 2097152 | bytes 4194308 | tf_op jit(solution)/shard_map/convert_element_type | solution.py:86
  (31 shorter events, 9.8 us)
Async XLA Ops:
  7.2 3.1 %copy-start.4 = (s32[768,1]{0,1:T(1,128)S(1)}, s32[768,1]{0,1:T(1,128)}, u32[]{:S(2)}) copy-start(s32[768,1]{0,1:T(1,128)} %param.7) | copy-start | bytes 9220
  7.2 85.7 %all-gather.2.cloned.1.call-start = ((), (), s32[]{:S(2)}) async-start(), calls=%async_computation.3 | async-start | bytes 6291456 | tf_op jit(solution)/shard_map/all_gather | solution.py:23
  10.3 1.1 copy-start.2
  26.1 11.9 %copy-start.3 = (bf16[768,512]{1,0:T(8,128)(2,1)S(1)}, bf16[768,512]{1,0:T(8,128)(2,1)}, u32[]{:S(2)}) copy-start(bf16[768,512]{1,0:T(8,128)(2,1)} %param.5) | copy-start | bytes 2359300
  26.1 36.2 %all-to-all-start.1 = ((bf16[4,64,6,512]{3,0,2,1:T(4,128)(2,1)}), bf16[4,64,6,512]{3,0,2,1:T(4,128)(2,1)}, u32[]{:S(2)}, u32[]{:S(2)}) async-start(bf16[4,64,6,512]{3,0,2,1:T(4,128)(2,1)} %copy.21), calls=%async_computation.1 | async-start | bytes 3145728 | tf_op jit(solution)/shard_map/all_to_all | solution.py:48
  62.4 28.2 %all-to-all-start = ((bf16[4,64,6,512]{3,0,2,1:T(4,128)(2,1)}), bf16[4,64,6,512]{3,0,2,1:T(4,128)(2,1)S(1)}, u32[]{:S(2)}, u32[]{:S(2)}) async-start(bf16[4,64,6,512]{3,0,2,1:T(4,128)(2,1)} %copy.20), calls=%async_computation | async-start | bytes 3145728 | tf_op jit(solution)/shard_map/all_to_all | solution.py:49
  67.5 79.5 %all-reduce.4.cloned.1.call-start = ((), (), s32[]{:S(2)}) async-start(), calls=%async_computation.4 | async-start | bytes 8388608 | tf_op jit(solution)/shard_map/psum | solution.py:84
  92.8 2.8 %copy-start = (f32[4,384,512]{2,0,1:T(4,128)S(1)}, f32[4,384,512]{2,0,1:T(4,128)}, u32[]{:S(2)}) copy-start(f32[4,384,512]{2,0,1:T(4,128)} %bitcast_convert_fusion) | copy-start | bytes 9437188
  99.8 2.2 %copy-start.1 = (bf16[4,2,512,512]{3,2,0,1:T(8,128)(2,1)S(1)}, bf16[4,2,512,512]{3,2,0,1:T(8,128)(2,1)}, u32[]{:S(2)}) copy-start(bf16[4,2,512,512]{3,2,0,1:T(8,128)(2,1)} %all-gather.2.cloned.1.call-done) | copy-start | bytes 12582916
  112.1 27.3 %all-to-all-start.2 = ((bf16[4,64,6,512]{3,0,2,1:T(4,128)(2,1)}), bf16[4,64,6,512]{3,0,2,1:T(4,128)(2,1)S(1)}, u32[]{:S(2)}, u32[]{:S(2)}) async-start(bf16[4,64,6,512]{3,0,2,1:T(4,128)(2,1)} %bitcast.4), calls=%async_computation.2 | async-start | bytes 3145728 | tf_op jit(solution)/shard_map/all_to_all | solution.py:74
Sparse Core Ops, SparseCore 0:
  10.4 18.7 all-gather.1
  107.2 29.7 all-reduce.3
where the time goes:
time: 158 us; the launch traced here: 157 us
  waiting for transfers between devices  55.3 us (35%)
  local copies, waits for them, and re-layouts  44.9 us (28%)
  starting transfers between devices  22.2 us (14%)
  between operations  14.3 us (9%)
  matrix products  14.2 us (9%)
  other arithmetic  6.45 us (4%)
    all_to_all x1, waiting for transfers between devices, on_device(): lax.all_to_all(grad.reshape(local_count, owner_count, capacity, feat_coun...  22.4 us
    all_to_all x1, waiting for transfers between devices, on_device(): lax.all_to_all(cots_buf, 'expert', split_axis=1, concat_axis=1, tiled=True)  19.8 us
    all_to_all x1, waiting for transfers between devices, on_device(): lax.all_to_all(feats_buf, 'expert', split_axis=1, concat_axis=1, tiled=True)  13 us
    all_to_all x1, starting transfers between devices, on_device(): lax.all_to_all(feats_buf, 'expert', split_axis=1, concat_axis=1, tiled=True)  11.9 us
    dot_general x2, matrix products, on_device(): jnp.einsum('lrd,ldk->lrk', acts[-1], full_weights[:, layer], preferred_el...  6.96 us
    unnamed x12, local copies, waits for them, and re-layouts  6 us
    reshape x2, local copies, waits for them, and re-layouts, on_device(): jnp.concatenate([samples, zero_row], 0)[source]  5.76 us
    reshape x2, local copies, waits for them, and re-layouts, on_device(): jnp.concatenate([cotangent, zero_row], 0)[source]  5.73 us
  transfers between devices with their start and end apart: 5, of which 3 were waited for; matrix products, arithmetic and copies ran while one was open for 28% of the time, Pallas kernels for 0%

commit v1 on v0

v1 whole, which is shorter than its diff:
```python
import functools
import math

import jax
import jax.numpy as jnp
import numpy as np
from jax import lax
from jax.experimental import pallas as pl
from jax.experimental.pallas import tpu as pltpu
from jax.sharding import PartitionSpec as P

MESH = pl.DeviceIdType.MESH
ROWS = 768
FEAT = 512
HALF = 256
EXPERTS = 256
LOCAL = 4
CAP = 6
PAIR = LOCAL * CAP
MSG = 2 * PAIR
PEERS = 64
GROUP = 16
GROUPS = PEERS // GROUP
BLOCK = 8
BLOCKS = GROUP // BLOCK
GROUP_ROWS = GROUP * CAP
EXPERT_ROWS = PEERS * CAP


def sort_matrices():
    into = np.zeros((BLOCK * MSG, BLOCK * MSG), np.float32)
    back = np.zeros((BLOCK * PAIR, BLOCK * PAIR), np.float32)
    for msg in range(BLOCK):
        for kind in range(2):
            for local in range(LOCAL):
                for slot in range(CAP):
                    by_expert = local * BLOCK * CAP + msg * CAP + slot
                    by_message = local * CAP + slot
                    into[kind * BLOCK * PAIR + by_expert, msg * MSG + kind * PAIR + by_message] = 1
                    if kind == 0:
                        back[msg * PAIR + by_message, by_expert] = 1
    return into, back


def dot(a, b):
    return jnp.dot(a, b, preferred_element_type=jnp.float32)


def dot_t(a, b):
    return lax.dot_general(a, b, (((1,), (1,)), ((), ())), preferred_element_type=jnp.float32)


def t_dot(a, b):
    return lax.dot_general(a, b, (((0,), (0,)), ((), ())), preferred_element_type=jnp.float32)


def kernel(
    norm_scale,
    ids_ref,
    into_ref,
    back_ref,
    samples_ref,
    cot_ref,
    weights_ref,
    grads_ref,
    wgrads_ref,
    send_buf,
    recv_buf,
    ysend_buf,
    yrecv_buf,
    x_group,
    g_group,
    y_group,
    act0,
    act1,
    pre0,
    pre1,
    wfull,
    wg_own,
    wg_send,
    wg_recv,
    target_col,
    acc,
    send_sem,
    recv_sem,
    ysend_sem,
    yrecv_sem,
    wlocal_sem,
    wsend_sem,
    wrecv_sem,
    gsend_sem,
    grecv_sem,
):
    me = lax.axis_index("expert")
    node = lax.axis_index("node")
    my_x = lax.rem(me, 4)
    my_y = lax.rem(lax.div(me, 4), 4)
    my_z = lax.div(me, 16)

    def shifted(pos, sign):
        dx = lax.rem(pos, 4)
        dy = lax.rem(lax.div(pos, 4), 4)
        dz = lax.rem(lax.div(pos, 16) + dx + dy, 4)
        px = lax.rem(my_x + sign * dx + 4, 4)
        py = lax.rem(my_y + sign * dy + 4, 4)
        pz = lax.rem(my_z + sign * dz + 4, 4)
        return pz * 16 + py * 4 + px

    barrier = pltpu.get_barrier_semaphore()

    def greet(pos, carry):
        pl.semaphore_signal(
            barrier, inc=1, device_id=(shifted(pos, 1), node), device_id_type=MESH
        )
        return carry

    lax.fori_loop(1, PEERS, greet, 0)
    pl.semaphore_signal(barrier, inc=1, device_id=(me, 1 - node), device_id_type=MESH)

    my_half = pl.ds(pl.multiple_of(node * HALF, HALF), HALF)
    w_local = pltpu.make_async_copy(weights_ref, wfull.at[:, :, my_half, :], wlocal_sem)
    w_local.start()
    w_remote = pltpu.make_async_remote_copy(
        src_ref=weights_ref,
        dst_ref=wfull.at[:, :, my_half, :],
        send_sem=wsend_sem,
        recv_sem=wrecv_sem,
        device_id=(me, 1 - node),
        device_id_type=MESH,
    )

    ids = ids_ref[...]
    onehot = lax.broadcasted_iota(jnp.int32, (EXPERTS, ROWS), 0) == ids
    before = lax.broadcasted_iota(jnp.int32, (ROWS, ROWS), 0) < lax.broadcasted_iota(
        jnp.int32, (ROWS, ROWS), 1
    )
    earlier = dot(onehot.astype(jnp.bfloat16), before.astype(jnp.bfloat16))
    slot = jnp.sum(jnp.where(onehot, earlier, 0.0), axis=0, keepdims=True).astype(jnp.int32)
    owner = ids >> 2
    dx = ((owner & 3) - my_x + 4) & 3
    dy = (((owner >> 2) & 3) - my_y + 4) & 3
    dz = ((owner >> 4) - my_z + 4) & 3
    pos_of = ((dz - dx - dy + 8) & 3) * 16 + dy * 4 + dx
    target = pos_of * PAIR + (ids & 3) * CAP + slot
    target_col[...] = jnp.broadcast_to(target.astype(jnp.float32), (128, ROWS)).T

    def message(pos):
        return pltpu.make_async_remote_copy(
            src_ref=send_buf.at[pos],
            dst_ref=recv_buf.at[pos],
            send_sem=send_sem.at[pos],
            recv_sem=recv_sem.at[pos],
            device_id=(shifted(pos, 1), node),
            device_id_type=MESH,
        )

    def reply(pos):
        return pltpu.make_async_remote_copy(
            src_ref=ysend_buf.at[pos],
            dst_ref=yrecv_buf.at[pos],
            send_sem=ysend_sem.at[pos],
            recv_sem=yrecv_sem.at[pos],
            device_id=(shifted(pos, -1), node),
            device_id_type=MESH,
        )

    def over(low, high, action):
        def step(pos, carry):
            action(pos)
            return carry

        lax.fori_loop(low, high, step, 0)

    def first_of(group):
        return jnp.where(group == 0, 1, group * GROUP)

    pl.semaphore_wait(barrier, PEERS)

    def dispatch(group, carry):
        rows = lax.broadcasted_iota(jnp.int32, (GROUP * PAIR, ROWS), 0) + group * (GROUP * PAIR)
        pick = (rows == target).astype(jnp.bfloat16)
        feats = dot(pick, samples_ref[...])
        cots = dot(pick, cot_ref[...])
        for j in range(GROUP):
            part = slice(j * PAIR, (j + 1) * PAIR)
            both = jnp.concatenate([feats[part], cots[part]], 0).astype(jnp.bfloat16)
            send_buf[group * GROUP + j] = both
            if j == 0:

                @pl.when(group == 0)
                def _():
                    recv_buf[0] = both

        over(first_of(group), (group + 1) * GROUP, lambda pos: message(pos).start())

        @pl.when(group == 0)
        def _():
            w_remote.start()

        return carry

    lax.fori_loop(0, GROUPS, dispatch, 0)
    w_local.wait()
    w_remote.wait()

    def slope(val, sig):
        return sig * (1.0 + val * (1.0 - sig))

    def compute(group, carry):
        over(first_of(group), (group + 1) * GROUP, lambda pos: message(pos).wait_recv())
        for block in range(BLOCKS):
            start = group * GROUP + block * BLOCK
            received = recv_buf[pl.ds(start, BLOCK)].reshape(BLOCK * MSG, FEAT)
            ordered = dot(into_ref[...], received).astype(jnp.bfloat16)
            size = BLOCK * CAP
            for local in range(LOCAL):
                x_group[local, block * size : (block + 1) * size] = ordered[
                    local * size : (local + 1) * size
                ]
                g_group[local, block * size : (block + 1) * size] = ordered[
                    BLOCK * PAIR + local * size : BLOCK * PAIR + (local + 1) * size
                ]
        rows = pl.ds(pl.multiple_of(group * GROUP_ROWS, GROUP_ROWS), GROUP_ROWS)

        def expert(local, inner):
            feats = x_group[local]
            act0[local, rows] = feats
            val0 = dot(feats, wfull[local, 0])
            sig0 = jax.nn.sigmoid(val0)
            hidden = (val0 * sig0).astype(jnp.bfloat16)
            act1[local, rows] = hidden
            val1 = dot(hidden, wfull[local, 1])
            sig1 = jax.nn.sigmoid(val1)
            grad1 = (g_group[local].astype(jnp.float32) * slope(val1, sig1)).astype(jnp.bfloat16)
            pre1[local, rows] = grad1
            back1 = dot_t(grad1, wfull[local, 1]).astype(jnp.bfloat16).astype(jnp.float32)
            grad0 = (back1 * slope(val0, sig0)).astype(jnp.bfloat16)
            pre0[local, rows] = grad0
            y_group[local] = dot_t(grad0, wfull[local, 0]).astype(jnp.bfloat16)
            return inner

        lax.fori_loop(0, LOCAL, expert, 0)
        for block in range(BLOCKS):
            size = BLOCK * CAP
            by_expert = y_group[:, block * size : (block + 1) * size].reshape(BLOCK * PAIR, FEAT)
            by_message = dot(back_ref[...], by_expert)
            for j in range(BLOCK):
                part = slice(j * PAIR, (j + 1) * PAIR)
                both = jnp.concatenate([by_message[part, :HALF], by_message[part, HALF:]], 0)
                both = both.astype(jnp.bfloat16)
                ysend_buf[group * GROUP + block * BLOCK + j] = both
                if block == 0 and j == 0:

                    @pl.when(group == 0)
                    def _():
                        yrecv_buf[0] = both

        over(first_of(group), (group + 1) * GROUP, lambda pos: reply(pos).start())
        return carry

    lax.fori_loop(0, GROUPS, compute, 0)

    other_half = pl.ds(pl.multiple_of((1 - node) * HALF, HALF), HALF)

    def wg_copy(local):
        return pltpu.make_async_remote_copy(
            src_ref=wg_send.at[local],
            dst_ref=wg_recv.at[local],
            send_sem=gsend_sem.at[local],
            recv_sem=grecv_sem.at[local],
            device_id=(me, 1 - node),
            device_id_type=MESH,
        )

    def weight_grads(local, carry):
        for layer, (act, pre) in enumerate(((act0, pre0), (act1, pre1))):
            grad = pre[local]
            sent = t_dot(act[local, :, other_half], grad) * norm_scale
            wg_send[local, layer] = sent.astype(jnp.bfloat16)
            kept = t_dot(act[local, :, my_half], grad) * norm_scale
            wg_own[local, layer] = kept.astype(jnp.bfloat16)
        wg_copy(local).start()
        return carry

    lax.fori_loop(0, LOCAL, weight_grads, 0)

    def add_grads(local, carry):
        wg_copy(local).wait()
        total = wg_own[local].astype(jnp.float32) + wg_recv[local].astype(jnp.float32)
        wgrads_ref[local] = total.astype(jnp.bfloat16)
        return carry

    lax.fori_loop(0, LOCAL, add_grads, 0)

    acc[...] = jnp.zeros_like(acc)

    def combine(group, carry):
        over(first_of(group), (group + 1) * GROUP, lambda pos: reply(pos).wait_recv())
        received = yrecv_buf[pl.ds(group * GROUP, GROUP)].astype(jnp.float32)
        left = received[:, :PAIR].reshape(GROUP * PAIR, HALF)
        right = received[:, PAIR:].reshape(GROUP * PAIR, HALF)
        ordered = jnp.concatenate([left, right], 1).astype(jnp.bfloat16)
        columns = lax.broadcasted_iota(jnp.int32, (ROWS, GROUP * PAIR), 1) + group * (GROUP * PAIR)
        pick = (target_col[:, :1].astype(jnp.int32) == columns).astype(jnp.bfloat16)
        acc[...] += dot(pick, ordered)
        return carry

    lax.fori_loop(0, GROUPS, combine, 0)
    grads_ref[...] = acc[...].astype(jnp.bfloat16)

    over(1, PEERS, lambda pos: message(pos).wait_send())
    over(1, PEERS, lambda pos: reply(pos).wait_send())


def on_device(samples, cotangent, weights, expert_ids):
    bf16 = jnp.bfloat16
    into, back = sort_matrices()
    node_count = lax.axis_size("node")
    norm_scale = 1.0 / math.sqrt(ROWS * node_count / LOCAL)
    vmem = pl.BlockSpec(memory_space=pltpu.VMEM)
    return pl.pallas_call(
        functools.partial(kernel, norm_scale),
        out_shape=(
            jax.ShapeDtypeStruct((ROWS, FEAT), bf16),
            jax.ShapeDtypeStruct((LOCAL, 2, HALF, FEAT), bf16),
        ),
        in_specs=[vmem] * 5 + [pl.BlockSpec(memory_space=pl.ANY)],
        out_specs=(vmem, vmem),
        scratch_shapes=[
            pltpu.VMEM((PEERS, MSG, FEAT), bf16),
            pltpu.VMEM((PEERS, MSG, FEAT), bf16),
            pltpu.VMEM((PEERS, MSG, HALF), bf16),
            pltpu.VMEM((PEERS, MSG, HALF), bf16),
            pltpu.VMEM((LOCAL, GROUP_ROWS, FEAT), bf16),
            pltpu.VMEM((LOCAL, GROUP_ROWS, FEAT), bf16),
            pltpu.VMEM((LOCAL, GROUP_ROWS, FEAT), bf16),
            pltpu.VMEM((LOCAL, EXPERT_ROWS, FEAT), bf16),
            pltpu.VMEM((LOCAL, EXPERT_ROWS, FEAT), bf16),
            pltpu.VMEM((LOCAL, EXPERT_ROWS, FEAT), bf16),
            pltpu.VMEM((LOCAL, EXPERT_ROWS, FEAT), bf16),
            pltpu.VMEM((LOCAL, 2, FEAT, FEAT), bf16),
            pltpu.VMEM((LOCAL, 2, HALF, FEAT), bf16),
            pltpu.VMEM((LOCAL, 2, HALF, FEAT), bf16),
            pltpu.VMEM((LOCAL, 2, HALF, FEAT), bf16),
            pltpu.VMEM((ROWS, 128), jnp.float32),
            pltpu.VMEM((ROWS, FEAT), jnp.float32),
            pltpu.SemaphoreType.DMA((PEERS,)),
            pltpu.SemaphoreType.DMA((PEERS,)),
            pltpu.SemaphoreType.DMA((PEERS,)),
            pltpu.SemaphoreType.DMA((PEERS,)),
            pltpu.SemaphoreType.DMA,
            pltpu.SemaphoreType.DMA,
            pltpu.SemaphoreType.DMA,
            pltpu.SemaphoreType.DMA((LOCAL,)),
            pltpu.SemaphoreType.DMA((LOCAL,)),
        ],
        compiler_params=pltpu.CompilerParams(
            collective_id=0, has_side_effects=True, vmem_limit_bytes=52 * 1024 * 1024
        ),
    )(
        expert_ids.reshape(1, ROWS),
        jnp.asarray(into, bf16),
        jnp.asarray(back, bf16),
        samples,
        cotangent,
        weights,
    )


def solution(mesh):
    return jax.shard_map(
        on_device,
        mesh=mesh,
        in_specs=(
            P(("expert", "node"), None),
            P(("expert", "node"), None),
            P("expert", None, "node", None),
            P(("expert", "node"), None),
        ),
        out_specs=(P(("expert", "node"), None), P("expert", None, "node", None)),
        check_vma=False,
    )
```

time: 158 us -> 87.5 us (0.55)
  Pallas kernels: 0 us -> 77.6 us
  waiting for transfers between devices: 55.3 us -> 0 us
  local copies, waits for them, and re-layouts: 44.9 us -> 7.59 us
  starting transfers between devices: 22.2 us -> 0 us
  matrix products: 14.2 us -> 0 us
  between operations: 14.3 us -> 0.65 us
  other arithmetic: 6.45 us -> 0 us
    pallas_call x0 -> x1, Pallas kernels: none -> 77.6 us  [on_device(): pl.pallas_call(functools.partial(kernel, norm_scale), out_shape=(jax.Shap...]
    all_to_all x3 -> x0, waiting for transfers between devices: 55.2 us -> none  [the longest x1 22.4 us: on_device(): lax.all_to_all(grad.reshape(local_count, owner_count, capacity, feat_coun...]
    all_to_all x3 -> x0, starting transfers between devices: 21.9 us -> none  [the longest x1 11.9 us: on_device(): lax.all_to_all(feats_buf, 'expert', split_axis=1, concat_axis=1, tiled=True)]
    reshape x6 -> x0, local copies, waits for them, and re-layouts: 17.1 us -> none  [the longest x2 5.76 us: on_device(): jnp.concatenate([samples, zero_row], 0)[source]]
    gather x3 -> x0, local copies, waits for them, and re-layouts: 14.2 us -> none  [the longest x1 5.45 us: on_device(): jnp.concatenate([cotangent, zero_row], 0)[source]]
    dot_general x7 -> x0, matrix products: 14.2 us -> none  [the longest x2 6.96 us: on_device(): jnp.einsum('lrd,ldk->lrk', acts[-1], full_weights[:, layer], preferred_el...]
    convert_element_type x3 -> x0, other arithmetic: 4.07 us -> none  [the longest x1 2.25 us: on_device(): grad.astype(jnp.float32) * silu_slope(preacts[layer])]
    scatter x1 -> x0, local copies, waits for them, and re-layouts: 3.38 us -> none  [on_device(): source = jnp.full((buffer_rows,), row_count, jnp.int32).at[target].set(jn...]
  transfers between devices with their start and end apart: 5 -> 0, of which waited for: 3 -> 0; matrix products, arithmetic and copies ran while one was open for 28% -> 0% of each run, Pallas kernels for 0% -> 0%
where the time goes in v1:
time: 87.5 us; the launch traced here: 85.9 us
  Pallas kernels  77.6 us (89%)
  local copies, waits for them, and re-layouts  7.59 us (9%)
    pallas_call x1, Pallas kernels, on_device(): pl.pallas_call(functools.partial(kernel, norm_scale), out_shape=(jax.Shap...  77.6 us
    unnamed x10, local copies, waits for them, and re-layouts  7.59 us

profile of v1, /device:TPU:0, one launch (start us, length us, event | category | flops | bytes accessed | tf_op | source)
XLA Modules:
  0.0 85.9 jit_solution(10787752277411251724)
XLA Ops:
  0.6 0.0 copy-start
  0.6 1.1 %copy-done = bf16[768,512]{1,0:T(8,128)(2,1)S(1)} copy-done((bf16[768,512]{1,0:T(8,128)(2,1)S(1)}, bf16[768,512]{1,0:T(8,128)(2,1)}, u32[]{:S(2)}) %copy-start) | copy-done | bytes 786456
  1.8 0.0 copy-start.1
  1.8 1.0 %copy-done.1 = bf16[384,384]{1,0:T(8,128)(2,1)S(1)} copy-done((bf16[384,384]{1,0:T(8,128)(2,1)S(1)}, bf16[384,384]{1,0:T(8,128)(2,1)}, u32[]{:S(2)}) %copy-start.1) | copy-done | bytes 294936
  2.7 0.0 copy-start.2
  2.7 0.9 %copy-done.2 = bf16[192,192]{1,0:T(8,128)(2,1)S(1)} copy-done((bf16[192,192]{1,0:T(8,128)(2,1)S(1)}, bf16[192,192]{1,0:T(8,128)(2,1)}, u32[]{:S(2)}) %copy-start.2) | copy-done | bytes 73752
  3.6 0.0 copy-start.3
  3.6 0.7 copy-done.3
  4.3 77.6 %shard_map.77 = (bf16[768,512]{1,0:T(8,128)(2,1)S(1)}, bf16[4,2,256,512]{3,2,1,0:T(8,128)(2,1)}) custom-call(s32[1,768]{1,0:T(1,128)S(1)} %bitcast.1, bf16[384,384]{1,0:T(8,128)(2,1)S(1)} %copy-done.1, bf16[192,192]{1,0:T(8,128)(2,1)S(1)} %copy-done.2, bf16[768,512]{1,0:T(8,128)(2,1)S(1)} %copy-done, bf16[768,512]{1,0:T(8,128)(2,1)} %cot_ref.1, ...), custom_call_target="tpu_custom_call" | custom-call | tf_op jit(solution)/shard_map/pallas_call | solution.py:321
  82.0 0.9 %copy.10 = bf16[768,512]{1,0:T(8,128)(2,1)} copy(bf16[768,512]{1,0:T(8,128)(2,1)S(1)} %get-tuple-element.4) | data formatting | bytes 1572864
  82.8 3.0 %copy.11 = bf16[4,2,256,512]{3,2,1,0:T(8,128)(2,1)} copy(bf16[4,2,256,512]{3,2,1,0:T(8,128)(2,1)} %get-tuple-element.5) | data formatting | bytes 4194304
Async XLA Ops:
  0.6 1.1 %copy-start = (bf16[768,512]{1,0:T(8,128)(2,1)S(1)}, bf16[768,512]{1,0:T(8,128)(2,1)}, u32[]{:S(2)}) copy-start(bf16[768,512]{1,0:T(8,128)(2,1)} %samples_ref.1) | copy-start | bytes 2359300
  1.8 1.0 %copy-start.1 = (bf16[384,384]{1,0:T(8,128)(2,1)S(1)}, bf16[384,384]{1,0:T(8,128)(2,1)}, u32[]{:S(2)}) copy-start(bf16[384,384]{1,0:T(8,128)(2,1)} %constant.4.clone.into_ref) | copy-start | bytes 884740
  2.7 0.9 %copy-start.2 = (bf16[192,192]{1,0:T(8,128)(2,1)S(1)}, bf16[192,192]{1,0:T(8,128)(2,1)}, u32[]{:S(2)}) copy-start(bf16[192,192]{1,0:T(8,128)(2,1)} %constant.5.clone.back_ref) | copy-start | bytes 221188
  3.6 0.7 copy-start.3

commit v2 on v1

--- a/solution.py
+++ b/solution.py
@@ -3,7 +3,6 @@
 
 import jax
 import jax.numpy as jnp
-import numpy as np
 from jax import lax
 from jax.experimental import pallas as pl
 from jax.experimental.pallas import tpu as pltpu
@@ -27,19 +26,28 @@
 EXPERT_ROWS = PEERS * CAP
 
 
-def sort_matrices():
-    into = np.zeros((BLOCK * MSG, BLOCK * MSG), np.float32)
-    back = np.zeros((BLOCK * PAIR, BLOCK * PAIR), np.float32)
-    for msg in range(BLOCK):
-        for kind in range(2):
-            for local in range(LOCAL):
-                for slot in range(CAP):
-                    by_expert = local * BLOCK * CAP + msg * CAP + slot
-                    by_message = local * CAP + slot
-                    into[kind * BLOCK * PAIR + by_expert, msg * MSG + kind * PAIR + by_message] = 1
-                    if kind == 0:
-                        back[msg * PAIR + by_message, by_expert] = 1
-    return into, back
+def sort_matrix():
+    size = BLOCK * MSG
+    row = lax.broadcasted_iota(jnp.int32, (1, size), 1)
+    msg = sum((row >= (k + 1) * MSG).astype(jnp.int32) for k in range(BLOCK - 1))
+    rest = row - msg * MSG
+    kind = (rest >= PAIR).astype(jnp.int32)
+    rest = rest - kind * PAIR
+    local = sum((rest >= (k + 1) * CAP).astype(jnp.int32) for k in range(LOCAL - 1))
+    slot = rest - local * CAP
+    place = kind * (BLOCK * PAIR) + local * (BLOCK * CAP) + msg * CAP + slot
+    return (lax.broadcasted_iota(jnp.int32, (size, size), 0) == place).astype(jnp.bfloat16)
+
+
+def unsort_matrix():
+    size = BLOCK * PAIR
+    row = lax.broadcasted_iota(jnp.int32, (1, size), 1)
+    local = sum((row >= (k + 1) * BLOCK * CAP).astype(jnp.int32) for k in range(LOCAL - 1))
+    rest = row - local * (BLOCK * CAP)
+    msg = sum((rest >= (k + 1) * CAP).astype(jnp.int32) for k in range(BLOCK - 1))
+    slot = rest - msg * CAP
+    place = msg * PAIR + local * CAP + slot
+    return (lax.broadcasted_iota(jnp.int32, (size, size), 0) == place).astype(jnp.bfloat16)
 
 
 def dot(a, b):
@@ -56,14 +64,17 @@
 
 def kernel(
     norm_scale,
-    ids_ref,
-    into_ref,
-    back_ref,
-    samples_ref,
-    cot_ref,
+    ids_hbm,
+    samples_hbm,
+    cot_hbm,
     weights_ref,
     grads_ref,
     wgrads_ref,
+    ids_ref,
+    samples_ref,
+    cot_ref,
+    into_ref,
+    back_ref,
     send_buf,
     recv_buf,
     ysend_buf,
@@ -79,8 +90,11 @@
     wg_own,
     wg_send,
     wg_recv,
+    wg_out,
+    g_out,
     target_col,
     acc,
+    in_sem,
     send_sem,
     recv_sem,
     ysend_sem,
@@ -90,6 +104,8 @@
     wrecv_sem,
     gsend_sem,
     grecv_sem,
+    out_sem,
+    gout_sem,
 ):
     me = lax.axis_index("expert")
     node = lax.axis_index("node")
@@ -106,15 +122,20 @@
         pz = lax.rem(my_z + sign * dz + 4, 4)
         return pz * 16 + py * 4 + px
 
+    loads = [
+        pltpu.make_async_copy(src, dst, in_sem.at[k])
+        for k, (src, dst) in enumerate(
+            ((ids_hbm, ids_ref), (samples_hbm, samples_ref), (cot_hbm, cot_ref))
+        )
+    ]
+    for load in loads:
+        load.start()
     barrier = pltpu.get_barrier_semaphore()
 
-    def greet(pos, carry):
-        pl.semaphore_signal(
-            barrier, inc=1, device_id=(shifted(pos, 1), node), device_id_type=MESH
-        )
-        return carry
-
-    lax.fori_loop(1, PEERS, greet, 0)
+    for step in range(1, PEERS):
+        peer = 16 * ((my_z + step // 16) & 3) + 4 * ((my_y + step // 4 % 4) & 3)
+        peer = peer + ((my_x + step % 4) & 3)
+        pl.semaphore_signal(barrier, inc=1, device_id=(peer, node), device_id_type=MESH)
     pl.semaphore_signal(barrier, inc=1, device_id=(me, 1 - node), device_id_type=MESH)
 
     my_half = pl.ds(pl.multiple_of(node * HALF, HALF), HALF)
@@ -129,6 +150,7 @@
         device_id_type=MESH,
     )
 
+    loads[0].wait()
     ids = ids_ref[...]
     onehot = lax.broadcasted_iota(jnp.int32, (EXPERTS, ROWS), 0) == ids
     before = lax.broadcasted_iota(jnp.int32, (ROWS, ROWS), 0) < lax.broadcasted_iota(
@@ -142,7 +164,6 @@
     dz = ((owner >> 4) - my_z + 4) & 3
     pos_of = ((dz - dx - dy + 8) & 3) * 16 + dy * 4 + dx
     target = pos_of * PAIR + (ids & 3) * CAP + slot
-    target_col[...] = jnp.broadcast_to(target.astype(jnp.float32), (128, ROWS)).T
 
     def message(pos):
         return pltpu.make_async_remote_copy(
@@ -174,9 +195,10 @@
     def first_of(group):
         return jnp.where(group == 0, 1, group * GROUP)
 
-    pl.semaphore_wait(barrier, PEERS)
-
-    def dispatch(group, carry):
+    loads[1].wait()
+    loads[2].wait()
+
+    def build(group):
         rows = lax.broadcasted_iota(jnp.int32, (GROUP * PAIR, ROWS), 0) + group * (GROUP * PAIR)
         pick = (rows == target).astype(jnp.bfloat16)
         feats = dot(pick, samples_ref[...])
@@ -185,21 +207,22 @@
             part = slice(j * PAIR, (j + 1) * PAIR)
             both = jnp.concatenate([feats[part], cots[part]], 0).astype(jnp.bfloat16)
             send_buf[group * GROUP + j] = both
-            if j == 0:
-
-                @pl.when(group == 0)
-                def _():
-                    recv_buf[0] = both
-
-        over(first_of(group), (group + 1) * GROUP, lambda pos: message(pos).start())
-
-        @pl.when(group == 0)
-        def _():
-            w_remote.start()
-
+
+    build(0)
+    recv_buf[0] = send_buf[0]
+    pl.semaphore_wait(barrier, PEERS)
+    over(1, GROUP, lambda pos: message(pos).start())
+    w_remote.start()
+
+    def dispatch(group, carry):
+        build(group)
+        over(group * GROUP, (group + 1) * GROUP, lambda pos: message(pos).start())
         return carry
 
-    lax.fori_loop(0, GROUPS, dispatch, 0)
+    lax.fori_loop(1, GROUPS, dispatch, 0)
+    into_ref[...] = sort_matrix()
+    back_ref[...] = unsort_matrix()
+    target_col[...] = jnp.broadcast_to(target.astype(jnp.float32), (128, ROWS)).T
     w_local.wait()
     w_remote.wait()
 
@@ -284,10 +307,14 @@
 
     lax.fori_loop(0, LOCAL, weight_grads, 0)
 
+    def wg_store(local):
+        return pltpu.make_async_copy(wg_out.at[local], wgrads_ref.at[local], out_sem.at[local])
+
     def add_grads(local, carry):
         wg_copy(local).wait()
         total = wg_own[local].astype(jnp.float32) + wg_recv[local].astype(jnp.float32)
-        wgrads_ref[local] = total.astype(jnp.bfloat16)
+        wg_out[local] = total.astype(jnp.bfloat16)
+        wg_store(local).start()
         return carry
 
     lax.fori_loop(0, LOCAL, add_grads, 0)
@@ -306,27 +333,56 @@
         return carry
 
     lax.fori_loop(0, GROUPS, combine, 0)
-    grads_ref[...] = acc[...].astype(jnp.bfloat16)
-
+    g_out[...] = acc[...].astype(jnp.bfloat16)
+    g_store = pltpu.make_async_copy(g_out, grads_ref, gout_sem)
+    g_store.start()
     over(1, PEERS, lambda pos: message(pos).wait_send())
     over(1, PEERS, lambda pos: reply(pos).wait_send())
+    over(0, LOCAL, lambda local: wg_store(local).wait())
+    g_store.wait()
+
+
+def hand_over(grads_in, wgrads_in, grads_out, wgrads_out, grads_buf, wgrads_buf, in_sem, out_sem):
+    half = ROWS // 2
+    parts = [
+        (src.at[part], buf.at[part], dst.at[part])
+        for src, buf, dst, all_parts in (
+            (wgrads_in, wgrads_buf, wgrads_out, range(LOCAL)),
+            (grads_in, grads_buf, grads_out, [pl.ds(k * half, half) for k in range(2)]),
+        )
+        for part in all_parts
+    ]
+    reads = [pltpu.make_async_copy(p[0], p[1], in_sem.at[k]) for k, p in enumerate(parts)]
+    writes = [pltpu.make_async_copy(p[1], p[2], out_sem.at[k]) for k, p in enumerate(parts)]
+    for copy in reads:
+        copy.start()
+    for read, write in zip(reads, writes):
+        read.wait()
+        write.start()
+    for copy in writes:
+        copy.wait()
 
 
 def on_device(samples, cotangent, weights, expert_ids):
     bf16 = jnp.bfloat16
-    into, back = sort_matrices()
     node_count = lax.axis_size("node")
     norm_scale = 1.0 / math.sqrt(ROWS * node_count / LOCAL)
-    vmem = pl.BlockSpec(memory_space=pltpu.VMEM)
-    return pl.pallas_call(
+    hbm = pl.BlockSpec(memory_space=pltpu.HBM)
+    outs = (
+        jax.ShapeDtypeStruct((ROWS, FEAT), bf16),
+        jax.ShapeDtypeStruct((LOCAL, 2, HALF, FEAT), bf16),
+    )
+    results = pl.pallas_call(
         functools.partial(kernel, norm_scale),
-        out_shape=(
-            jax.ShapeDtypeStruct((ROWS, FEAT), bf16),
-            jax.ShapeDtypeStruct((LOCAL, 2, HALF, FEAT), bf16),
-        ),
-        in_specs=[vmem] * 5 + [pl.BlockSpec(memory_space=pl.ANY)],
-        out_specs=(vmem, vmem),
+        out_shape=outs,
+        in_specs=[hbm] * 4,
+        out_specs=(hbm, hbm),
         scratch_shapes=[
+            pltpu.VMEM((1, ROWS), jnp.int32),
+            pltpu.VMEM((ROWS, FEAT), bf16),
+            pltpu.VMEM((ROWS, FEAT), bf16),
+            pltpu.VMEM((BLOCK * MSG, BLOCK * MSG), bf16),
+            pltpu.VMEM((BLOCK * PAIR, BLOCK * PAIR), bf16),
             pltpu.VMEM((PEERS, MSG, FEAT), bf16),
             pltpu.VMEM((PEERS, MSG, FEAT), bf16),
             pltpu.VMEM((PEERS, MSG, HALF), bf16),
@@ -342,8 +398,11 @@
             pltpu.VMEM((LOCAL, 2, HALF, FEAT), bf16),
             pltpu.VMEM((LOCAL, 2, HALF, FEAT), bf16),
             pltpu.VMEM((LOCAL, 2, HALF, FEAT), bf16),
+            pltpu.VMEM((LOCAL, 2, HALF, FEAT), bf16),
+            pltpu.VMEM((ROWS, FEAT), bf16),
             pltpu.VMEM((ROWS, 128), jnp.float32),
             pltpu.VMEM((ROWS, FEAT), jnp.float32),
+            pltpu.SemaphoreType.DMA((3,)),
             pltpu.SemaphoreType.DMA((PEERS,)),
             pltpu.SemaphoreType.DMA((PEERS,)),
             pltpu.SemaphoreType.DMA((PEERS,)),
@@ -353,18 +412,31 @@
             pltpu.SemaphoreType.DMA,
             pltpu.SemaphoreType.DMA((LOCAL,)),
             pltpu.SemaphoreType.DMA((LOCAL,)),
+            pltpu.SemaphoreType.DMA((LOCAL,)),
+            pltpu.SemaphoreType.DMA,
         ],
         compiler_params=pltpu.CompilerParams(
-            collective_id=0, has_side_effects=True, vmem_limit_bytes=52 * 1024 * 1024
+            collective_id=0, has_side_effects=True, vmem_limit_bytes=60 * 1024 * 1024
         ),
     )(
         expert_ids.reshape(1, ROWS),
-        jnp.asarray(into, bf16),
-        jnp.asarray(back, bf16),
         samples,
         cotangent,
         weights,
     )
+    return pl.pallas_call(
+        hand_over,
+        out_shape=outs,
+        in_specs=[hbm] * 2,
+        out_specs=(hbm, hbm),
+        scratch_shapes=[
+            pltpu.VMEM((ROWS, FEAT), bf16),
+            pltpu.VMEM((LOCAL, 2, HALF, FEAT), bf16),
+            pltpu.SemaphoreType.DMA((LOCAL + 2,)),
+            pltpu.SemaphoreType.DMA((LOCAL + 2,)),
+        ],
+        compiler_params=pltpu.CompilerParams(vmem_limit_bytes=60 * 1024 * 1024),
+    )(*results)
 
 
 def solution(mesh):

time: 87.5 us -> 78.5 us (0.90)
  local copies, waits for them, and re-layouts: 7.59 us -> 0 us
  Pallas kernels: 77.6 us -> 76.4 us
    unnamed x10 -> x0, local copies, waits for them, and re-layouts: 7.59 us -> none
    pallas_call x1 -> x2, Pallas kernels: 77.6 us -> 76.4 us  [the longest x1 73.6 us: on_device(): pl.pallas_call(functools.partial(kernel, norm_scale), out_shape=outs, in_...]
where the time goes in v2:
time: 78.5 us; the launch traced here: 77 us
  Pallas kernels  76.4 us (97%)
    pallas_call x1, Pallas kernels, on_device(): pl.pallas_call(functools.partial(kernel, norm_scale), out_shape=outs, in_...  73.6 us
    pallas_call x1, Pallas kernels, on_device(): pl.pallas_call(hand_over, out_shape=outs, in_specs=[hbm] * 2, out_specs=(...  2.71 us

profile of v2, /device:TPU:0, one launch (start us, length us, event | category | flops | bytes accessed | tf_op | source)
XLA Modules:
  0.0 77.0 jit_solution(10535012098846142740)
XLA Ops:
  0.6 73.6 %shard_map.59 = (bf16[768,512]{1,0:T(8,128)(2,1)}, bf16[4,2,256,512]{3,2,1,0:T(8,128)(2,1)}) custom-call(s32[1,768]{1,0:T(1,128)} %bitcast.1, bf16[768,512]{1,0:T(8,128)(2,1)} %samples_hbm.1, bf16[768,512]{1,0:T(8,128)(2,1)} %cot_hbm.1, bf16[4,2,256,512]{3,2,1,0:T(8,128)(2,1)} %weights_ref.1), custom_call_target="tpu_custom_call" | custom-call | tf_op jit(solution)/shard_map/pallas_call | solution.py:375
  74.3 2.7 %shard_map.60 = (bf16[768,512]{1,0:T(8,128)(2,1)}, bf16[4,2,256,512]{3,2,1,0:T(8,128)(2,1)}) custom-call(bf16[768,512]{1,0:T(8,128)(2,1)} %get-tuple-element.4.grads_in, bf16[4,2,256,512]{3,2,1,0:T(8,128)(2,1)} %get-tuple-element.5.wgrads_in), custom_call_target="tpu_custom_call" | custom-call | tf_op jit(solution)/shard_map/pallas_call | solution.py:427

commit v3 on v2

--- a/solution.py
+++ b/solution.py
@@ -20,7 +20,7 @@
 PEERS = 64
 GROUP = 16
 GROUPS = PEERS // GROUP
-BLOCK = 8
+BLOCK = 4
 BLOCKS = GROUP // BLOCK
 GROUP_ROWS = GROUP * CAP
 EXPERT_ROWS = PEERS * CAP
@@ -79,14 +79,14 @@
     recv_buf,
     ysend_buf,
     yrecv_buf,
-    x_group,
     g_group,
-    y_group,
+    slope0,
     act0,
     act1,
     pre0,
     pre1,
     wfull,
+    wg_acc,
     wg_own,
     wg_send,
     wg_recv,
@@ -231,57 +231,45 @@
 
     def compute(group, carry):
         over(first_of(group), (group + 1) * GROUP, lambda pos: message(pos).wait_recv())
+        size = BLOCK * CAP
+        ordered = []
         for block in range(BLOCKS):
-            start = group * GROUP + block * BLOCK
-            received = recv_buf[pl.ds(start, BLOCK)].reshape(BLOCK * MSG, FEAT)
-            ordered = dot(into_ref[...], received).astype(jnp.bfloat16)
-            size = BLOCK * CAP
-            for local in range(LOCAL):
-                x_group[local, block * size : (block + 1) * size] = ordered[
-                    local * size : (local + 1) * size
-                ]
-                g_group[local, block * size : (block + 1) * size] = ordered[
-                    BLOCK * PAIR + local * size : BLOCK * PAIR + (local + 1) * size
-                ]
+            received = recv_buf[pl.ds(group * GROUP + block * BLOCK, BLOCK)]
+            ordered.append(dot(into_ref[...], received.reshape(BLOCK * MSG, FEAT)))
+
+        def rows_of(place):
+            return jnp.concatenate([part[place * size : (place + 1) * size] for part in ordered], 0)
+
         rows = pl.ds(pl.multiple_of(group * GROUP_ROWS, GROUP_ROWS), GROUP_ROWS)
-
-        def expert(local, inner):
-            feats = x_group[local]
-            act0[local, rows] = feats
-            val0 = dot(feats, wfull[local, 0])
-            sig0 = jax.nn.sigmoid(val0)
-            hidden = (val0 * sig0).astype(jnp.bfloat16)
-            act1[local, rows] = hidden
-            val1 = dot(hidden, wfull[local, 1])
-            sig1 = jax.nn.sigmoid(val1)
-            grad1 = (g_group[local].astype(jnp.float32) * slope(val1, sig1)).astype(jnp.bfloat16)
-            pre1[local, rows] = grad1
-            back1 = dot_t(grad1, wfull[local, 1]).astype(jnp.bfloat16).astype(jnp.float32)
-            grad0 = (back1 * slope(val0, sig0)).astype(jnp.bfloat16)
-            pre0[local, rows] = grad0
-            y_group[local] = dot_t(grad0, wfull[local, 0]).astype(jnp.bfloat16)
-            return inner
-
-        lax.fori_loop(0, LOCAL, expert, 0)
+        experts = range(LOCAL)
+        for e in experts:
+            act0[e, rows] = rows_of(e).astype(jnp.bfloat16)
+            g_group[e] = rows_of(LOCAL + e)
+        val0 = [dot(act0[e, rows], wfull[e, 0]) for e in experts]
+        for e in experts:
+            sig = jax.nn.sigmoid(val0[e])
+            act1[e, rows] = (val0[e] * sig).astype(jnp.bfloat16)
+            slope0[e] = slope(val0[e], sig)
+        val1 = [dot(act1[e, rows], wfull[e, 1]) for e in experts]
+        for e in experts:
+            sig = jax.nn.sigmoid(val1[e])
+            pre1[e, rows] = (g_group[e] * slope(val1[e], sig)).astype(jnp.bfloat16)
+        back1 = [dot_t(pre1[e, rows], wfull[e, 1]) for e in experts]
+        for e in experts:
+            grad = back1[e].astype(jnp.bfloat16).astype(jnp.float32)
+            pre0[e, rows] = (grad * slope0[e]).astype(jnp.bfloat16)
+        back0 = [dot_t(pre0[e, rows], wfull[e, 0]) for e in experts]
         for block in range(BLOCKS):
-            size = BLOCK * CAP
-            by_expert = y_group[:, block * size : (block + 1) * size].reshape(BLOCK * PAIR, FEAT)
+            part = slice(block * size, (block + 1) * size)
+            by_expert = jnp.concatenate([back0[e][part] for e in experts], 0).astype(jnp.bfloat16)
             by_message = dot(back_ref[...], by_expert)
             for j in range(BLOCK):
                 part = slice(j * PAIR, (j + 1) * PAIR)
                 both = jnp.concatenate([by_message[part, :HALF], by_message[part, HALF:]], 0)
-                both = both.astype(jnp.bfloat16)
-                ysend_buf[group * GROUP + block * BLOCK + j] = both
-                if block == 0 and j == 0:
-
-                    @pl.when(group == 0)
-                    def _():
-                        yrecv_buf[0] = both
+                ysend_buf[group * GROUP + block * BLOCK + j] = both.astype(jnp.bfloat16)
 
         over(first_of(group), (group + 1) * GROUP, lambda pos: reply(pos).start())
         return carry
-
-    lax.fori_loop(0, GROUPS, compute, 0)
 
     other_half = pl.ds(pl.multiple_of((1 - node) * HALF, HALF), HALF)
 
@@ -295,17 +283,23 @@
             device_id_type=MESH,
         )
 
-    def weight_grads(local, carry):
-        for layer, (act, pre) in enumerate(((act0, pre0), (act1, pre1))):
-            grad = pre[local]
-            sent = t_dot(act[local, :, other_half], grad) * norm_scale
-            wg_send[local, layer] = sent.astype(jnp.bfloat16)
-            kept = t_dot(act[local, :, my_half], grad) * norm_scale
-            wg_own[local, layer] = kept.astype(jnp.bfloat16)
+    layers = ((act0, pre0), (act1, pre1))
+    span = EXPERT_ROWS // 2
+
+    def first_grads(local, carry):
+        for layer, (act, pre) in enumerate(layers):
+            wg_acc[local, layer] = t_dot(act[local, :span], pre[local, :span])
+        return carry
+
+    def last_grads(local, carry):
+        for layer, (act, pre) in enumerate(layers):
+            for half, result in ((other_half, wg_send), (my_half, wg_own)):
+                total = wg_acc[local, layer, half] + t_dot(
+                    act[local, span:, half], pre[local, span:]
+                )
+                result[local, layer] = (total * norm_scale).astype(jnp.bfloat16)
         wg_copy(local).start()
         return carry
-
-    lax.fori_loop(0, LOCAL, weight_grads, 0)
 
     def wg_store(local):
         return pltpu.make_async_copy(wg_out.at[local], wgrads_ref.at[local], out_sem.at[local])
@@ -317,7 +311,11 @@
         wg_store(local).start()
         return carry
 
-    lax.fori_loop(0, LOCAL, add_grads, 0)
+    lax.fori_loop(0, 2, compute, 0)
+    lax.fori_loop(0, LOCAL, first_grads, 0)
+    lax.fori_loop(2, GROUPS, compute, 0)
+    lax.fori_loop(0, LOCAL, last_grads, 0)
+    yrecv_buf[0] = ysend_buf[0]
 
     acc[...] = jnp.zeros_like(acc)
 
@@ -332,7 +330,9 @@
         acc[...] += dot(pick, ordered)
         return carry
 
-    lax.fori_loop(0, GROUPS, combine, 0)
+    lax.fori_loop(0, GROUPS - 1, combine, 0)
+    lax.fori_loop(0, LOCAL, add_grads, 0)
+    combine(GROUPS - 1, 0)
     g_out[...] = acc[...].astype(jnp.bfloat16)
     g_store = pltpu.make_async_copy(g_out, grads_ref, gout_sem)
     g_store.start()
@@ -387,14 +387,14 @@
             pltpu.VMEM((PEERS, MSG, FEAT), bf16),
             pltpu.VMEM((PEERS, MSG, HALF), bf16),
             pltpu.VMEM((PEERS, MSG, HALF), bf16),
-            pltpu.VMEM((LOCAL, GROUP_ROWS, FEAT), bf16),
-            pltpu.VMEM((LOCAL, GROUP_ROWS, FEAT), bf16),
-            pltpu.VMEM((LOCAL, GROUP_ROWS, FEAT), bf16),
+            pltpu.VMEM((LOCAL, GROUP_ROWS, FEAT), jnp.float32),
+            pltpu.VMEM((LOCAL, GROUP_ROWS, FEAT), jnp.float32),
             pltpu.VMEM((LOCAL, EXPERT_ROWS, FEAT), bf16),
             pltpu.VMEM((LOCAL, EXPERT_ROWS, FEAT), bf16),
             pltpu.VMEM((LOCAL, EXPERT_ROWS, FEAT), bf16),
             pltpu.VMEM((LOCAL, EXPERT_ROWS, FEAT), bf16),
             pltpu.VMEM((LOCAL, 2, FEAT, FEAT), bf16),
+            pltpu.VMEM((LOCAL, 2, FEAT, FEAT), jnp.float32),
             pltpu.VMEM((LOCAL, 2, HALF, FEAT), bf16),
             pltpu.VMEM((LOCAL, 2, HALF, FEAT), bf16),
             pltpu.VMEM((LOCAL, 2, HALF, FEAT), bf16),

time: 78.5 us -> 74.2 us (0.945); the launches traced: 77 us -> 74.1 us
  Pallas kernels: 76.4 us -> 73.5 us
    pallas_call x1, Pallas kernels: 73.6 us -> 70.7 us  [on_device(): pl.pallas_call(functools.partial(kernel, norm_scale), out_shape=outs, in_...]
where the time goes in v3:
time: 74.2 us; the launch traced here: 74.1 us
  Pallas kernels  73.5 us (99%)
    pallas_call x1, Pallas kernels, on_device(): pl.pallas_call(functools.partial(kernel, norm_scale), out_shape=outs, in_...  70.7 us
    pallas_call x1, Pallas kernels, on_device(): pl.pallas_call(hand_over, out_shape=outs, in_specs=[hbm] * 2, out_specs=(...  2.71 us

profile of v3, /device:TPU:0, one launch (start us, length us, event | category | flops | bytes accessed | tf_op | source)
XLA Modules:
  0.0 74.1 jit_solution(12136815096380883880)
XLA Ops:
  0.6 70.7 %shard_map.59 = (bf16[768,512]{1,0:T(8,128)(2,1)}, bf16[4,2,256,512]{3,2,1,0:T(8,128)(2,1)}) custom-call(s32[1,768]{1,0:T(1,128)} %bitcast.1, bf16[768,512]{1,0:T(8,128)(2,1)} %samples_hbm.1, bf16[768,512]{1,0:T(8,128)(2,1)} %cot_hbm.1, bf16[4,2,256,512]{3,2,1,0:T(8,128)(2,1)} %weights_ref.1), custom_call_target="tpu_custom_call" | custom-call | tf_op jit(solution)/shard_map/pallas_call | solution.py:375
  71.4 2.7 %shard_map.60 = (bf16[768,512]{1,0:T(8,128)(2,1)}, bf16[4,2,256,512]{3,2,1,0:T(8,128)(2,1)}) custom-call(bf16[768,512]{1,0:T(8,128)(2,1)} %get-tuple-element.4.grads_in, bf16[4,2,256,512]{3,2,1,0:T(8,128)(2,1)} %get-tuple-element.5.wgrads_in), custom_call_target="tpu_custom_call" | custom-call | tf_op jit(solution)/shard_map/pallas_call | solution.py:427

commit v4 on v3

--- a/solution.py
+++ b/solution.py
@@ -21,8 +21,9 @@
 GROUP = 16
 GROUPS = PEERS // GROUP
 BLOCK = 4
-BLOCKS = GROUP // BLOCK
+PASS = 16
 GROUP_ROWS = GROUP * CAP
+GRAD_PARTS = 4
 EXPERT_ROWS = PEERS * CAP
 
 
@@ -192,6 +193,16 @@
 
         lax.fori_loop(low, high, step, 0)
 
+    def send_all(copy, first, stride):
+        def send(j):
+            pos = first + lax.rem(j * stride, GROUP)
+
+            @pl.when(pos != 0)
+            def _():
+                copy(pos).start()
+
+        over(0, GROUP, send)
+
     def first_of(group):
         return jnp.where(group == 0, 1, group * GROUP)
 
@@ -211,12 +222,12 @@
     build(0)
     recv_buf[0] = send_buf[0]
     pl.semaphore_wait(barrier, PEERS)
-    over(1, GROUP, lambda pos: message(pos).start())
+    send_all(message, 0, 5)
     w_remote.start()
 
     def dispatch(group, carry):
         build(group)
-        over(group * GROUP, (group + 1) * GROUP, lambda pos: message(pos).start())
+        send_all(message, group * GROUP, 5)
         return carry
 
     lax.fori_loop(1, GROUPS, dispatch, 0)
@@ -229,47 +240,48 @@
     def slope(val, sig):
         return sig * (1.0 + val * (1.0 - sig))
 
-    def compute(group, carry):
-        over(first_of(group), (group + 1) * GROUP, lambda pos: message(pos).wait_recv())
+    def compute(count, first):
+        low = jnp.where(first == 0, 1, first)
+        over(low, first + count, lambda pos: message(pos).wait_recv())
         size = BLOCK * CAP
         ordered = []
-        for block in range(BLOCKS):
-            received = recv_buf[pl.ds(group * GROUP + block * BLOCK, BLOCK)]
+        for block in range(count // BLOCK):
+            received = recv_buf[pl.ds(first + block * BLOCK, BLOCK)]
             ordered.append(dot(into_ref[...], received.reshape(BLOCK * MSG, FEAT)))
 
         def rows_of(place):
             return jnp.concatenate([part[place * size : (place + 1) * size] for part in ordered], 0)
 
-        rows = pl.ds(pl.multiple_of(group * GROUP_ROWS, GROUP_ROWS), GROUP_ROWS)
+        rows = pl.ds(pl.multiple_of(first * CAP, 16), count * CAP)
+        kept = slice(0, count * CAP)
         experts = range(LOCAL)
         for e in experts:
             act0[e, rows] = rows_of(e).astype(jnp.bfloat16)
-            g_group[e] = rows_of(LOCAL + e)
+            g_group[e, kept] = rows_of(LOCAL + e)
         val0 = [dot(act0[e, rows], wfull[e, 0]) for e in experts]
         for e in experts:
             sig = jax.nn.sigmoid(val0[e])
             act1[e, rows] = (val0[e] * sig).astype(jnp.bfloat16)
-            slope0[e] = slope(val0[e], sig)
+            slope0[e, kept] = slope(val0[e], sig)
         val1 = [dot(act1[e, rows], wfull[e, 1]) for e in experts]
         for e in experts:
             sig = jax.nn.sigmoid(val1[e])
-            pre1[e, rows] = (g_group[e] * slope(val1[e], sig)).astype(jnp.bfloat16)
+            pre1[e, rows] = (g_group[e, kept] * slope(val1[e], sig)).astype(jnp.bfloat16)
         back1 = [dot_t(pre1[e, rows], wfull[e, 1]) for e in experts]
         for e in experts:
             grad = back1[e].astype(jnp.bfloat16).astype(jnp.float32)
-            pre0[e, rows] = (grad * slope0[e]).astype(jnp.bfloat16)
+            pre0[e, rows] = (grad * slope0[e, kept]).astype(jnp.bfloat16)
         back0 = [dot_t(pre0[e, rows], wfull[e, 0]) for e in experts]
-        for block in range(BLOCKS):
+        for block in range(count // BLOCK):
             part = slice(block * size, (block + 1) * size)
             by_expert = jnp.concatenate([back0[e][part] for e in experts], 0).astype(jnp.bfloat16)
             by_message = dot(back_ref[...], by_expert)
             for j in range(BLOCK):
                 part = slice(j * PAIR, (j + 1) * PAIR)
                 both = jnp.concatenate([by_message[part, :HALF], by_message[part, HALF:]], 0)
-                ysend_buf[group * GROUP + block * BLOCK + j] = both.astype(jnp.bfloat16)
-
-        over(first_of(group), (group + 1) * GROUP, lambda pos: reply(pos).start())
-        return carry
+                ysend_buf[first + block * BLOCK + j] = both.astype(jnp.bfloat16)
+
+        send_all(reply, first, 13)
 
     other_half = pl.ds(pl.multiple_of((1 - node) * HALF, HALF), HALF)
 
@@ -311,9 +323,14 @@
         wg_store(local).start()
         return carry
 
-    lax.fori_loop(0, 2, compute, 0)
-    lax.fori_loop(0, LOCAL, first_grads, 0)
-    lax.fori_loop(2, GROUPS, compute, 0)
+    def pass_of(step):
+        compute(PASS, step * PASS)
+
+        @pl.when(step == PEERS // PASS // 2 - 1)
+        def _():
+            lax.fori_loop(0, LOCAL, first_grads, 0)
+
+    over(0, PEERS // PASS, pass_of)
     lax.fori_loop(0, LOCAL, last_grads, 0)
     yrecv_buf[0] = ysend_buf[0]
 
@@ -343,12 +360,13 @@
 
 
 def hand_over(grads_in, wgrads_in, grads_out, wgrads_out, grads_buf, wgrads_buf, in_sem, out_sem):
-    half = ROWS // 2
+    size = ROWS // GRAD_PARTS
+    rows = [pl.ds(k * size, size) for k in range(GRAD_PARTS)]
     parts = [
         (src.at[part], buf.at[part], dst.at[part])
         for src, buf, dst, all_parts in (
-            (wgrads_in, wgrads_buf, wgrads_out, range(LOCAL)),
-            (grads_in, grads_buf, grads_out, [pl.ds(k * half, half) for k in range(2)]),
+            (wgrads_in, wgrads_buf, wgrads_out, [(k, j) for k in range(LOCAL) for j in range(2)]),
+            (grads_in, grads_buf, grads_out, rows),
         )
         for part in all_parts
     ]
@@ -432,8 +450,8 @@
         scratch_shapes=[
             pltpu.VMEM((ROWS, FEAT), bf16),
             pltpu.VMEM((LOCAL, 2, HALF, FEAT), bf16),
-            pltpu.SemaphoreType.DMA((LOCAL + 2,)),
-            pltpu.SemaphoreType.DMA((LOCAL + 2,)),
+            pltpu.SemaphoreType.DMA((2 * LOCAL + GRAD_PARTS,)),
+            pltpu.SemaphoreType.DMA((2 * LOCAL + GRAD_PARTS,)),
         ],
         compiler_params=pltpu.CompilerParams(vmem_limit_bytes=60 * 1024 * 1024),
     )(*results)

time: 74.2 us -> 70.9 us (0.956)
  Pallas kernels: 73.5 us -> 70.1 us
    pallas_call x1, Pallas kernels: 70.7 us -> 67.4 us  [on_device(): pl.pallas_call(functools.partial(kernel, norm_scale), out_shape=outs, in_...]
where the time goes in v4:
time: 70.9 us; the launch traced here: 70.8 us
  Pallas kernels  70.1 us (99%)
    pallas_call x1, Pallas kernels, on_device(): pl.pallas_call(functools.partial(kernel, norm_scale), out_shape=outs, in_...  67.4 us
    pallas_call x1, Pallas kernels, on_device(): pl.pallas_call(hand_over, out_shape=outs, in_specs=[hbm] * 2, out_specs=(...  2.72 us

profile of v4, /device:TPU:0, one launch (start us, length us, event | category | flops | bytes accessed | tf_op | source)
XLA Modules:
  0.0 70.8 jit_solution(9694517827451114283)
XLA Ops:
  0.6 67.4 %shard_map.59 = (bf16[768,512]{1,0:T(8,128)(2,1)}, bf16[4,2,256,512]{3,2,1,0:T(8,128)(2,1)}) custom-call(s32[1,768]{1,0:T(1,128)} %bitcast.1, bf16[768,512]{1,0:T(8,128)(2,1)} %samples_hbm.1, bf16[768,512]{1,0:T(8,128)(2,1)} %cot_hbm.1, bf16[4,2,256,512]{3,2,1,0:T(8,128)(2,1)} %weights_ref.1), custom_call_target="tpu_custom_call" | custom-call | tf_op jit(solution)/shard_map/pallas_call | solution.py:393
  68.1 2.7 %shard_map.60 = (bf16[768,512]{1,0:T(8,128)(2,1)}, bf16[4,2,256,512]{3,2,1,0:T(8,128)(2,1)}) custom-call(bf16[768,512]{1,0:T(8,128)(2,1)} %get-tuple-element.4.grads_in, bf16[4,2,256,512]{3,2,1,0:T(8,128)(2,1)} %get-tuple-element.5.wgrads_in), custom_call_target="tpu_custom_call" | custom-call | tf_op jit(solution)/shard_map/pallas_call | solution.py:445

commit v5 on v4

--- a/solution.py
+++ b/solution.py
@@ -170,8 +170,8 @@
         return pltpu.make_async_remote_copy(
             src_ref=send_buf.at[pos],
             dst_ref=recv_buf.at[pos],
-            send_sem=send_sem.at[pos],
-            recv_sem=recv_sem.at[pos],
+            send_sem=send_sem.at[pos // GROUP],
+            recv_sem=recv_sem.at[pos // GROUP],
             device_id=(shifted(pos, 1), node),
             device_id_type=MESH,
         )
@@ -180,8 +180,8 @@
         return pltpu.make_async_remote_copy(
             src_ref=ysend_buf.at[pos],
             dst_ref=yrecv_buf.at[pos],
-            send_sem=ysend_sem.at[pos],
-            recv_sem=yrecv_sem.at[pos],
+            send_sem=ysend_sem.at[pos // GROUP],
+            recv_sem=yrecv_sem.at[pos // GROUP],
             device_id=(shifted(pos, -1), node),
             device_id_type=MESH,
         )
@@ -203,8 +203,35 @@
 
         over(0, GROUP, send)
 
-    def first_of(group):
-        return jnp.where(group == 0, 1, group * GROUP)
+    def whole(group, first, count):
+        part = pl.ds(group * GROUP + first, count)
+        return (
+            pltpu.make_async_remote_copy(
+                src_ref=send_buf.at[part],
+                dst_ref=recv_buf.at[part],
+                send_sem=send_sem.at[group],
+                recv_sem=recv_sem.at[group],
+                device_id=(me, 1 - node),
+                device_id_type=MESH,
+            ),
+            pltpu.make_async_remote_copy(
+                src_ref=ysend_buf.at[part],
+                dst_ref=yrecv_buf.at[part],
+                send_sem=ysend_sem.at[group],
+                recv_sem=yrecv_sem.at[group],
+                device_id=(me, 1 - node),
+                device_id_type=MESH,
+            ),
+        )
+
+    def for_group(group, action):
+        @pl.when(group == 0)
+        def _():
+            action(*whole(group, 1, GROUP - 1))
+
+        @pl.when(group != 0)
+        def _():
+            action(*whole(group, 0, GROUP))
 
     loads[1].wait()
     loads[2].wait()
@@ -241,8 +268,7 @@
         return sig * (1.0 + val * (1.0 - sig))
 
     def compute(count, first):
-        low = jnp.where(first == 0, 1, first)
-        over(low, first + count, lambda pos: message(pos).wait_recv())
+        for_group(first // GROUP, lambda messages, replies: messages.wait_recv())
         size = BLOCK * CAP
         ordered = []
         for block in range(count // BLOCK):
@@ -337,7 +363,7 @@
     acc[...] = jnp.zeros_like(acc)
 
     def combine(group, carry):
-        over(first_of(group), (group + 1) * GROUP, lambda pos: reply(pos).wait_recv())
+        for_group(group, lambda messages, replies: replies.wait_recv())
         received = yrecv_buf[pl.ds(group * GROUP, GROUP)].astype(jnp.float32)
         left = received[:, :PAIR].reshape(GROUP * PAIR, HALF)
         right = received[:, PAIR:].reshape(GROUP * PAIR, HALF)
@@ -353,8 +379,12 @@
     g_out[...] = acc[...].astype(jnp.bfloat16)
     g_store = pltpu.make_async_copy(g_out, grads_ref, gout_sem)
     g_store.start()
-    over(1, PEERS, lambda pos: message(pos).wait_send())
-    over(1, PEERS, lambda pos: reply(pos).wait_send())
+
+    def drain(group):
+        for_group(group, lambda messages, replies: messages.wait_send())
+        for_group(group, lambda messages, replies: replies.wait_send())
+
+    over(0, GROUPS, drain)
     over(0, LOCAL, lambda local: wg_store(local).wait())
     g_store.wait()
 
@@ -421,10 +451,10 @@
             pltpu.VMEM((ROWS, 128), jnp.float32),
             pltpu.VMEM((ROWS, FEAT), jnp.float32),
             pltpu.SemaphoreType.DMA((3,)),
-            pltpu.SemaphoreType.DMA((PEERS,)),
-            pltpu.SemaphoreType.DMA((PEERS,)),
-            pltpu.SemaphoreType.DMA((PEERS,)),
-            pltpu.SemaphoreType.DMA((PEERS,)),
+            pltpu.SemaphoreType.DMA((GROUPS,)),
+            pltpu.SemaphoreType.DMA((GROUPS,)),
+            pltpu.SemaphoreType.DMA((GROUPS,)),
+            pltpu.SemaphoreType.DMA((GROUPS,)),
             pltpu.SemaphoreType.DMA,
             pltpu.SemaphoreType.DMA,
             pltpu.SemaphoreType.DMA,

time: 70.9 us -> 68.8 us (0.970)
  Pallas kernels: 70.1 us -> 68 us
    pallas_call x1, Pallas kernels: 67.4 us -> 65.3 us  [on_device(): pl.pallas_call(functools.partial(kernel, norm_scale), out_shape=outs, in_...]
where the time goes in v5:
time: 68.8 us; the launch traced here: 68.6 us
  Pallas kernels  68 us (99%)
    pallas_call x1, Pallas kernels, on_device(): pl.pallas_call(functools.partial(kernel, norm_scale), out_shape=outs, in_...  65.3 us
    pallas_call x1, Pallas kernels, on_device(): pl.pallas_call(hand_over, out_shape=outs, in_specs=[hbm] * 2, out_specs=(...  2.72 us

profile of v5, /device:TPU:0, one launch (start us, length us, event | category | flops | bytes accessed | tf_op | source)
XLA Modules:
  0.0 68.6 jit_solution(11069489922837746418)
XLA Ops:
  0.6 65.3 %shard_map.59 = (bf16[768,512]{1,0:T(8,128)(2,1)}, bf16[4,2,256,512]{3,2,1,0:T(8,128)(2,1)}) custom-call(s32[1,768]{1,0:T(1,128)} %bitcast.1, bf16[768,512]{1,0:T(8,128)(2,1)} %samples_hbm.1, bf16[768,512]{1,0:T(8,128)(2,1)} %cot_hbm.1, bf16[4,2,256,512]{3,2,1,0:T(8,128)(2,1)} %weights_ref.1), custom_call_target="tpu_custom_call" | custom-call | tf_op jit(solution)/shard_map/pallas_call | solution.py:423
  65.9 2.7 %shard_map.60 = (bf16[768,512]{1,0:T(8,128)(2,1)}, bf16[4,2,256,512]{3,2,1,0:T(8,128)(2,1)}) custom-call(bf16[768,512]{1,0:T(8,128)(2,1)} %get-tuple-element.4.grads_in, bf16[4,2,256,512]{3,2,1,0:T(8,128)(2,1)} %get-tuple-element.5.wgrads_in), custom_call_target="tpu_custom_call" | custom-call | tf_op jit(solution)/shard_map/pallas_call | solution.py:475

commit v6 on v5

--- a/solution.py
+++ b/solution.py
@@ -307,7 +307,7 @@
                 both = jnp.concatenate([by_message[part, :HALF], by_message[part, HALF:]], 0)
                 ysend_buf[first + block * BLOCK + j] = both.astype(jnp.bfloat16)
 
-        send_all(reply, first, 13)
+        send_all(reply, first, 9)
 
     other_half = pl.ds(pl.multiple_of((1 - node) * HALF, HALF), HALF)
 
@@ -362,7 +362,7 @@
 
     acc[...] = jnp.zeros_like(acc)
 
-    def combine(group, carry):
+    def combined(group):
         for_group(group, lambda messages, replies: replies.wait_recv())
         received = yrecv_buf[pl.ds(group * GROUP, GROUP)].astype(jnp.float32)
         left = received[:, :PAIR].reshape(GROUP * PAIR, HALF)
@@ -370,13 +370,15 @@
         ordered = jnp.concatenate([left, right], 1).astype(jnp.bfloat16)
         columns = lax.broadcasted_iota(jnp.int32, (ROWS, GROUP * PAIR), 1) + group * (GROUP * PAIR)
         pick = (target_col[:, :1].astype(jnp.int32) == columns).astype(jnp.bfloat16)
-        acc[...] += dot(pick, ordered)
+        return dot(pick, ordered)
+
+    def combine(group, carry):
+        acc[...] += combined(group)
         return carry
 
     lax.fori_loop(0, GROUPS - 1, combine, 0)
     lax.fori_loop(0, LOCAL, add_grads, 0)
-    combine(GROUPS - 1, 0)
-    g_out[...] = acc[...].astype(jnp.bfloat16)
+    g_out[...] = (acc[...] + combined(GROUPS - 1)).astype(jnp.bfloat16)
     g_store = pltpu.make_async_copy(g_out, grads_ref, gout_sem)
     g_store.start()
 

time: 68.8 us -> 68.1 us (0.990)
  Pallas kernels: 68 us -> 67.3 us
where the time goes in v6:
time: 68.1 us; the launch traced here: 67.9 us
  Pallas kernels  67.3 us (99%)
    pallas_call x1, Pallas kernels, on_device(): pl.pallas_call(functools.partial(kernel, norm_scale), out_shape=outs, in_...  64.6 us
    pallas_call x1, Pallas kernels, on_device(): pl.pallas_call(hand_over, out_shape=outs, in_specs=[hbm] * 2, out_specs=(...  2.72 us

profile of v6, /device:TPU:0, one launch (start us, length us, event | category | flops | bytes accessed | tf_op | source)
XLA Modules:
  0.0 67.9 jit_solution(4956726839450638036)
XLA Ops:
  0.6 64.6 %shard_map.59 = (bf16[768,512]{1,0:T(8,128)(2,1)}, bf16[4,2,256,512]{3,2,1,0:T(8,128)(2,1)}) custom-call(s32[1,768]{1,0:T(1,128)} %bitcast.1, bf16[768,512]{1,0:T(8,128)(2,1)} %samples_hbm.1, bf16[768,512]{1,0:T(8,128)(2,1)} %cot_hbm.1, bf16[4,2,256,512]{3,2,1,0:T(8,128)(2,1)} %weights_ref.1), custom_call_target="tpu_custom_call" | custom-call | tf_op jit(solution)/shard_map/pallas_call | solution.py:425
  65.2 2.7 %shard_map.60 = (bf16[768,512]{1,0:T(8,128)(2,1)}, bf16[4,2,256,512]{3,2,1,0:T(8,128)(2,1)}) custom-call(bf16[768,512]{1,0:T(8,128)(2,1)} %get-tuple-element.4.grads_in, bf16[4,2,256,512]{3,2,1,0:T(8,128)(2,1)} %get-tuple-element.5.wgrads_in), custom_call_target="tpu_custom_call" | custom-call | tf_op jit(solution)/shard_map/pallas_call | solution.py:477

commit v7 on v6

--- a/solution.py
+++ b/solution.py
@@ -194,14 +194,12 @@
         lax.fori_loop(low, high, step, 0)
 
     def send_all(copy, first, stride):
-        def send(j):
-            pos = first + lax.rem(j * stride, GROUP)
-
-            @pl.when(pos != 0)
-            def _():
-                copy(pos).start()
-
-        over(0, GROUP, send)
+        @pl.when(first != 0)
+        def _():
+            copy(first).start()
+
+        for j in range(1, GROUP):
+            copy(first + j * stride % GROUP).start()
 
     def whole(group, first, count):
         part = pl.ds(group * GROUP + first, count)

time: 68.1 us -> 68.1 us (level)
  no operation moved by 1% of the time
where the time goes in v7:
time: 68.1 us; the launch traced here: 67.9 us
  Pallas kernels  67.3 us (99%)
    pallas_call x1, Pallas kernels, on_device(): pl.pallas_call(functools.partial(kernel, norm_scale), out_shape=outs, in_...  64.6 us
    pallas_call x1, Pallas kernels, on_device(): pl.pallas_call(hand_over, out_shape=outs, in_specs=[hbm] * 2, out_specs=(...  2.72 us

profile of v7, /device:TPU:0, one launch (start us, length us, event | category | flops | bytes accessed | tf_op | source)
XLA Modules:
  0.0 67.9 jit_solution(1705553731410059171)
XLA Ops:
  0.6 64.6 %shard_map.59 = (bf16[768,512]{1,0:T(8,128)(2,1)}, bf16[4,2,256,512]{3,2,1,0:T(8,128)(2,1)}) custom-call(s32[1,768]{1,0:T(1,128)} %bitcast.1, bf16[768,512]{1,0:T(8,128)(2,1)} %samples_hbm.1, bf16[768,512]{1,0:T(8,128)(2,1)} %cot_hbm.1, bf16[4,2,256,512]{3,2,1,0:T(8,128)(2,1)} %weights_ref.1), custom_call_target="tpu_custom_call" | custom-call | tf_op jit(solution)/shard_map/pallas_call | solution.py:423
  65.2 2.7 %shard_map.60 = (bf16[768,512]{1,0:T(8,128)(2,1)}, bf16[4,2,256,512]{3,2,1,0:T(8,128)(2,1)}) custom-call(bf16[768,512]{1,0:T(8,128)(2,1)} %get-tuple-element.4.grads_in, bf16[4,2,256,512]{3,2,1,0:T(8,128)(2,1)} %get-tuple-element.5.wgrads_in), custom_call_target="tpu_custom_call" | custom-call | tf_op jit(solution)/shard_map/pallas_call | solution.py:475
